TPU v7x, 32 devices: a whole 2x2x4 slice. The times are simulated.
32 devices in a mesh: head: 2 (over y), replica: 16 (over z, x, core).
Axes of the slice: x: 2, y: 2, z: 4, core: 2. Of those that a mesh axis runs over, the one named last changes fastest.
Arguments:
- queries: bfloat16 [16, 256, 512], P('replica', None, 'head'), may hold values from -1.5 to 1.5
- keys: bfloat16 [16, 256, 512], P('replica', None, 'head'), may hold values from -1.5 to 1.5
- values: bfloat16 [16, 256, 512], P('replica', None, 'head'), may hold values from -6 to 6
- out_weight: bfloat16 [4096, 512], P('replica', 'head'), may hold values from -0.25 to 0.25
- cotangent: bfloat16 [16, 256, 4096], P('replica'), may hold values from -6 to 6
- on_time: int32 [16], P('replica'), may hold values from 0 to 1, as said below
Outputs:
- layer_out: bfloat16 [16, 256, 4096], P('replica')
- value_grad: bfloat16 [16, 256, 512], P('replica', None, 'head')
- weight_grad: float32 [4096, 512], P('replica', 'head')
Inputs may be any that keep to these rules, and one draw needn't show every extreme that they name: `on_time`: at least one replica is on time.
All inputs are finite; a program needn't handle non-finite values.
Results may differ from a plain program's by a relative error of at most 0.022.
Values may be sent and summed in bfloat16 or wider, within the bound.
A program may use at most 64 MiB of HBM per device.

v0:
```python
import jax
import jax.numpy as jnp
from jax import lax
from jax.sharding import PartitionSpec as P


def local(queries, keys, values, out_weight, cotangent, on_time):
    query_rows = queries[0]
    key_rows = keys[0]
    value_rows = values[0]
    cot_rows = cotangent[0]
    tokens = query_rows.shape[0]
    head_float = lax.axis_index("head").astype(jnp.float32)
    gamma = 1.0 - 2.0 ** (-5.0 - head_float)
    position = jnp.arange(tokens)
    offset = (position[:, None] - position[None, :]).astype(jnp.float32)
    decay = jnp.where(offset >= 0.0, jnp.exp(jnp.maximum(offset, 0.0) * jnp.log(gamma)), 0.0)
    scores = (
        lax.dot_general(
            query_rows, key_rows, (((1,), (1,)), ((), ())), preferred_element_type=jnp.float32
        )
        * decay
    )
    denom = jnp.maximum(jnp.sum(jnp.abs(scores), axis=-1, keepdims=True), 1.0)
    weights = (scores / denom).astype(jnp.bfloat16)
    mixed = jnp.dot(weights, value_rows, preferred_element_type=jnp.float32).astype(jnp.bfloat16)
    full_weight = lax.all_gather(out_weight, "replica", axis=0, tiled=True)
    accepted = lax.psum(on_time, "replica").astype(jnp.float32)
    masked = mixed * on_time[0].astype(jnp.bfloat16)
    term = lax.dot_general(
        mixed, full_weight, (((1,), (1,)), ((), ())), preferred_element_type=jnp.float32
    )
    layer_out = lax.psum(term.astype(jnp.bfloat16), "head")
    summed = lax.psum_scatter(
        lax.dot_general(
            cot_rows, masked, (((0,), (0,)), ((), ())), preferred_element_type=jnp.float32
        ),
        "replica",
        scatter_dimension=0,
        tiled=True,
    )
    mixed_grad = jnp.dot(cot_rows, full_weight, preferred_element_type=jnp.float32).astype(
        jnp.bfloat16
    )
    value_grad = lax.dot_general(
        weights, mixed_grad, (((0,), (0,)), ((), ())), preferred_element_type=jnp.float32
    ).astype(jnp.bfloat16)
    weight_grad = summed / accepted
    return (layer_out[None], value_grad[None], weight_grad)


def solution(mesh):
    return jax.shard_map(
        local,
        mesh=mesh,
        in_specs=(
            P("replica", None, "head"),
            P("replica", None, "head"),
            P("replica", None, "head"),
            P("replica", "head"),
            P("replica", None, None),
            P("replica"),
        ),
        out_specs=(P("replica", None, None), P("replica", None, "head"), P("replica", "head")),
        check_vma=False,
    )
```

profile of v0, /device:TPU:0, one launch (start us, length us, event | category | flops | bytes accessed | tf_op | source)
XLA Modules:
  0.0 204.0 jit_solution(16956256186491411154)
XLA Ops:
  7.2 0.0 copy-start
  7.2 0.0 all-gather.2.cloned.1.call-start
  7.2 0.7 all-gather.2.cloned.1.call-update
  7.9 0.0 reduce-scatter.2.cloned.1.call-start
  8.7 1.2 abs_reduce_fusion
  9.9 1.1 convolution_convert_fusion.2
  11.1 0.0 copy-done
  11.1 2.7 %convolution_bitcast_fusion = f32[4096,256]{0,1:T(8,128)} fusion(bf16[1,256,4096]{2,1,0:T(8,128)(2,1)S(1)} %copy-done, bf16[256,256]{1,0:T(8,128)(2,1)S(1)} %convolution_convert_fusion.2, bf16[]{:T(256)} %bitcast.6), kind=kOutput, calls=%fused_computation | convolution fusion | flops 536936448 | bytes 6422530 | tf_op jit(solution)/shard_map/dot_general | solution.py:35
  13.8 0.0 reduce-scatter.2.cloned.1.call-update
  13.8 0.0 all-reduce.2.cloned.1.call-start
  13.8 40.5 %all-gather.2.cloned.1.call-done = bf16[4096,256]{1,0:T(8,128)(2,1)} async-done(((bf16[256,256]{1,0:T(8,128)(2,1)}), bf16[4096,256]{1,0:T(8,128)(2,1)}) %all-gather.2.cloned.1.call-update) | async-done | bytes 2097168 | tf_op jit(solution)/shard_map/all_gather | solution.py:27
  54.3 3.7 %fusion = bf16[1,256,4096]{2,1,0:T(8,128)(2,1)} fusion(bf16[256,256]{1,0:T(8,128)(2,1)S(1)} %convolution_convert_fusion.2, bf16[4096,256]{1,0:T(8,128)(2,1)} %all-gather.2.cloned.1.call-done), kind=kOutput, calls=%fused_computation.2 | convolution fusion | flops 537919488 | bytes 4325376 | tf_op jit(solution)/shard_map/dot_general | solution.py:30
  58.0 0.0 all-reduce.2.cloned.1.call-update
  58.0 10.8 %psum.15 = s32[1]{0:T(128)} all-reduce(s32[1]{0:T(128)} %param.11), channel_id=1, replica_groups=mesh['head'=2,'replica'=16] {'replica'}, use_global_device_ids=true, to_apply=%region_3.4 | all-reduce | flops 1 | bytes 8 | tf_op jit(solution)/shard_map/psum | solution.py:28
  69.4 3.3 %fusion.7 = bf16[1,256,256]{2,1,0:T(8,128)(2,1)} fusion(bf16[4096,256]{1,0:T(8,128)(2,1)} %all-gather.2.cloned.1.call-done, bf16[1,256,4096]{2,1,0:T(8,128)(2,1)S(1)} %copy-done, f32[256,256]{0,1:T(8,128)S(1)} %get-tuple-element.7, f32[256]{0:T(256)S(1)} %broadcast_maximum_fusion), kind=kOutput, calls=%fused_computation.10 | convolution fusion | flops 570687488 | bytes 4588544 | tf_op jit(solution)/shard_map/dot_general | solution.py:45
  72.7 56.7 %reduce-scatter.2.cloned.1.call-done = f32[256,256]{0,1:T(8,128)} async-done(((f32[4096,256]{0,1:T(8,128)}), f32[256,256]{0,1:T(8,128)}) %reduce-scatter.2.cloned.1.call-update) | async-done | bytes 262160 | tf_op jit(solution)/shard_map/reduce_scatter | solution.py:34
  129.3 1.0 broadcast_divide_fusion
  130.3 0.8 copy.9
  131.2 63.2 %all-reduce.2.cloned.1.call-done = bf16[1,256,4096]{2,1,0:T(8,128)(2,1)} async-done(((bf16[1,256,4096]{2,1,0:T(8,128)(2,1)}), bf16[1,256,4096]{2,1,0:T(8,128)(2,1)}) %all-reduce.2.cloned.1.call-update) | async-done | bytes 2097168 | tf_op jit(solution)/shard_map/psum | solution.py:33
  194.3 3.1 %copy.12 = bf16[1,256,4096]{2,1,0:T(8,128)(2,1)} copy(bf16[1,256,4096]{2,1,0:T(8,128)(2,1)} %all-reduce.2.cloned.1.call-done) | data formatting | bytes 4194304
  (1 shorter events, 0.0 us)
Async XLA Ops:
  7.2 3.9 %copy-start = (bf16[1,256,4096]{2,1,0:T(8,128)(2,1)S(1)}, bf16[1,256,4096]{2,1,0:T(8,128)(2,1)}, u32[]{:S(2)}) copy-start(bf16[1,256,4096]{2,1,0:T(8,128)(2,1)} %param.10) | copy-start | bytes 6291460
  7.2 47.1 %all-gather.2.cloned.1.call-start = ((), (), s32[]{:S(2)}) async-start(), calls=%async_computation.1 | async-start | bytes 2228224 | tf_op jit(solution)/shard_map/all_gather | solution.py:27
  7.9 121.4 %reduce-scatter.2.cloned.1.call-start = ((), (), s32[]{:S(2)}) async-start(), calls=%async_computation.3 | async-start | bytes 4456448 | tf_op jit(solution)/shard_map/reduce_scatter | solution.py:34
  13.8 180.5 %all-reduce.2.cloned.1.call-start = ((), (), s32[]{:S(2)}) async-start(), calls=%async_computation.2 | async-start | bytes 4194304 | tf_op jit(solution)/shard_map/psum | solution.py:33
Sparse Core Ops, SparseCore 0:
  10.2 44.0 all-gather.1
  58.2 71.1 reduce-scatter.1
  132.3 61.9 all-reduce.1
where the time goes:
time: 204 us
  waiting for transfers between devices  161 us (79%)
  between operations  15.2 us (7%)
  matrix products  12 us (6%)
  blocking collectives  10.8 us (5%)
  local copies, waits for them, and re-layouts  3.97 us (2%)
    psum x1, waiting for transfers between devices, local(): layer_out = lax.psum(term.astype(jnp.bfloat16), 'head')  63.2 us
    reduce_scatter x1, waiting for transfers between devices, local(): lax.psum_scatter(lax.dot_general(cot_rows, masked, (((0,), (0,)), ((), ()...  56.7 us
    all_gather x1, waiting for transfers between devices, local(): full_weight = lax.all_gather(out_weight, 'replica', axis=0, tiled=True)  40.5 us
    psum x1, blocking collectives, local(): accepted = lax.psum(on_time, 'replica').astype(jnp.float32)  10.8 us
  transfers between devices with their start and end apart: 3, of which 3 were waited for; matrix products, arithmetic and copies ran while one was open for 7% of the time, Pallas kernels for 0%

commit v1 on v0

v1 whole, which is shorter than its diff:
```python
import functools
import math

import jax
import jax.numpy as jnp
from jax import lax
from jax.experimental import pallas as pl
from jax.experimental.pallas import tpu as pltpu
from jax.sharding import PartitionSpec as P

MESH = pl.DeviceIdType.MESH
FLAG_ROWS = 16
F32 = jnp.float32
BF16 = jnp.bfloat16


def dot(a, b, dims):
    return lax.dot_general(a, b, ((dims[:1], dims[1:]), ((), ())), preferred_element_type=F32)


def each(count, body):
    if count <= 4:
        for i in range(count):
            body(i)
    else:
        lax.fori_loop(0, count, lambda i, c: (body(i), c)[1], 0)


def when(cond, body):
    if isinstance(cond, bool):
        if cond:
            body()
    else:
        pl.when(cond)(body)


def kernel(
    heads, replicas,
    q_hbm, k_hbm, v_hbm, w_hbm, cot_hbm, on_ref,
    layer_hbm, value_grad_ref, weight_grad_ref,
    q, k, v, cot, layer, w_all, mixed_all, mixed_grad, part, weights_ref,
    core_out, core_in, x_out, x_in, z_out, up_in, down_in,
    load_sem, layer_sem,
    w_recv, up_send, down_send, x_send, head_send, core_send,
    mixed_send, mixed_recv,
    core_out_sem, core_in_sem, x_out_sem, x_in_sem, z_out_sem, up_sem, down_sem,
):
    depth = replicas // 4
    rows = w_hbm.shape[0]
    group = 4 * rows
    tokens = q.shape[0]
    head = lax.axis_index("head")
    me = lax.axis_index("replica")
    z, x, c = me // 4, (me // 2) % 2, me % 2

    def rep(zz, xx, cc):
        return zz * 4 + xx * 2 + cc

    sibling = (head, rep(z, x, 1 - c))
    across = (head, rep(z, 1 - x, c))
    above = (head, rep(z + 1, x, c))
    below = (head, rep(z - 1, x, c))

    def peer(j):
        return lax.rem(head + 1 + j, heads)

    barrier = pltpu.get_barrier_semaphore()

    def greet(device):
        pl.semaphore_signal(barrier, inc=1, device_id=device, device_id_type=MESH)

    greet(sibling)
    greet(across)
    each(heads - 1, lambda j: greet((peer(j), me)))
    pl.when(z > 0)(lambda: greet(below))
    pl.when(z < depth - 1)(lambda: greet(above))

    loads = [
        pltpu.make_async_copy(src, dst, load_sem.at[i])
        for i, (src, dst) in enumerate(
            ((q_hbm.at[0], q), (k_hbm.at[0], k), (v_hbm.at[0], v), (cot_hbm.at[0], cot),
             (w_hbm, w_all.at[head, pl.ds(pl.multiple_of(me * rows, rows), rows)]))
        )
    ]
    for load in loads:
        load.start()
    pl.semaphore_wait(
        barrier, 1 + heads + jnp.where(z > 0, 1, 0) + jnp.where(z < depth - 1, 1, 0)
    )

    def block(hh, rr):
        return w_all.at[hh, pl.ds(pl.multiple_of(rr * rows, rows), rows)]

    def w_copy(hh, rr, sem, device, src=None):
        return pltpu.make_async_remote_copy(
            src_ref=block(hh, rr) if src is None else src,
            dst_ref=block(hh, rr),
            send_sem=sem,
            recv_sem=w_recv.at[hh, rr],
            device_id=device,
            device_id_type=MESH,
        )

    def w_wait(hh, rr):
        w_copy(hh, rr, core_send.at[hh, rr], sibling).wait_recv()

    def to_above(rr, src=None):
        return w_copy(head, rr, up_send.at[rr], above, src)

    def to_below(rr, src=None):
        return w_copy(head, rr, down_send.at[rr], below, src)

    def to_across(rr, src=None):
        return w_copy(head, rr, x_send.at[rr], across, src)

    def to_peer(j, rr, src=None):
        return w_copy(head, rr, head_send.at[j, rr], (peer(j), me), src)

    def to_core(hh, rr, src=None):
        return w_copy(hh, rr, core_send.at[hh, rr], sibling, src)

    def spread(rr, src=None):
        each(heads - 1, lambda j: to_peer(j, rr, src).start())
        to_core(head, rr, src).start()

    pl.when(z < depth - 1)(lambda: to_above(me, w_hbm).start())
    pl.when(z > 0)(lambda: to_below(me, w_hbm).start())
    to_across(me, w_hbm).start()
    spread(me, w_hbm)

    def around(d, body):
        if isinstance(d, int) and d == 0:
            body(z, None)
        else:
            pl.when(z - d >= 0)(lambda: body(z - d, True))
            pl.when(z + d < depth)(lambda: body(z + d, False))

    def gather_z(d):
        def body(zz, went_up):
            rr = rep(zz, x, c)
            w_wait(head, rr)
            if went_up:
                pl.when(z < depth - 1)(lambda: to_above(rr).start())
            else:
                pl.when(z > 0)(lambda: to_below(rr).start())
            to_across(rr).start()
            spread(rr)

        around(d, body)

    def gather_x(d):
        def body(zz, _):
            rr = rep(zz, 1 - x, c)
            w_wait(head, rr)
            spread(rr)

        around(d, body)

    def gather_heads(d):
        def body(zz, _):
            def from_peer(j):
                for xx in (x, 1 - x):
                    rr = rep(zz, xx, c)
                    w_wait(peer(j), rr)
                    to_core(peer(j), rr).start()

            each(heads - 1, from_peer)

        around(d, body)

    def core_wait(hh, zz):
        for xx in (0, 1):
            w_wait(hh, rep(zz, xx, 1 - c))

    for load in loads[:3]:
        load.wait()
    row = lax.broadcasted_iota(jnp.int32, (tokens, tokens), 0)
    col = lax.broadcasted_iota(jnp.int32, (tokens, tokens), 1)
    offset = (row - col).astype(F32)
    log_gamma = jnp.float32(math.log(1.0 - 2.0 ** -5.0))
    for i in range(1, heads):
        log_gamma = jnp.where(head == i, jnp.float32(math.log(1.0 - 2.0 ** (-5.0 - i))), log_gamma)
    decay = jnp.where(offset >= 0.0, jnp.exp(jnp.maximum(offset, 0.0) * log_gamma), 0.0)
    scores = dot(q[...], k[...], (1, 1)) * decay
    denom = jnp.maximum(jnp.sum(jnp.abs(scores), axis=-1, keepdims=True), 1.0)
    weights_ref[...] = (scores / denom).astype(BF16)
    mixed_all[head] = dot(weights_ref[...], v[...], (1, 0)).astype(BF16)

    def mixed_copy(j):
        return pltpu.make_async_remote_copy(
            src_ref=mixed_all.at[head],
            dst_ref=mixed_all.at[head],
            send_sem=mixed_send.at[j],
            recv_sem=mixed_recv.at[head],
            device_id=(peer(j), me),
            device_id_type=MESH,
        )

    def mixed_wait(j):
        pltpu.make_async_remote_copy(
            src_ref=mixed_all.at[peer(j)],
            dst_ref=mixed_all.at[peer(j)],
            send_sem=mixed_send.at[j],
            recv_sem=mixed_recv.at[peer(j)],
            device_id=(peer(j), me),
            device_id_type=MESH,
        ).wait_recv()

    each(heads - 1, lambda j: mixed_copy(j).start())

    on = on_ref[0].astype(F32)
    flags = jnp.full((FLAG_ROWS, part.shape[1]), 1.0, F32) * on
    body_rows = pl.ds(0, rows)
    flag_rows = pl.ds(rows, FLAG_ROWS)

    def order(i):
        if isinstance(i, int):
            return i // 2 if i % 2 == 0 else depth - 1 - i // 2
        return jnp.where(i % 2 == 0, i // 2, depth - 1 - i // 2)

    def own_part(rr):
        return part[pl.ds(pl.multiple_of(rr * rows, rows), rows)]

    def core_copy(slot):
        return pltpu.make_async_remote_copy(
            core_out.at[slot], core_in.at[slot], core_out_sem.at[slot], core_in_sem.at[slot],
            device_id=sibling, device_id_type=MESH,
        )

    def x_copy(zz):
        return pltpu.make_async_remote_copy(
            x_out.at[zz], x_in.at[zz], x_out_sem.at[zz], x_in_sem.at[zz],
            device_id=across, device_id_type=MESH,
        )

    def up_copy(zz):
        return pltpu.make_async_remote_copy(
            z_out.at[zz], up_in.at[zz], z_out_sem.at[zz], up_sem.at[zz],
            device_id=above, device_id_type=MESH,
        )

    def down_copy(zz):
        return pltpu.make_async_remote_copy(
            z_out.at[zz], down_in.at[zz], z_out_sem.at[zz], down_sem.at[zz],
            device_id=below, device_id_type=MESH,
        )

    loads[3].wait()
    masked = mixed_all[head] * on.astype(BF16)

    def sum_start(i):
        zz = order(i)
        at = pl.multiple_of(zz * group, group)
        part[pl.ds(at, group)] = dot(cot[:, pl.ds(at, group)], masked, (0, 0))
        for xx in (1 - x, x):
            slot = zz * 2 + xx
            core_out[slot, body_rows] = own_part(rep(zz, xx, 1 - c)).astype(BF16)
            core_out[slot, flag_rows] = flags.astype(BF16)
            core_copy(slot).start()

    def sum_x(i):
        zz = order(i)
        slot = zz * 2 + 1 - x
        core_copy(slot).wait_recv()
        x_out[zz, body_rows] = (
            own_part(rep(zz, 1 - x, c)) + core_in[slot, body_rows].astype(F32)
        ).astype(BF16)
        x_out[zz, flag_rows] = (flags + core_in[slot, flag_rows].astype(F32)).astype(BF16)
        x_copy(zz).start()

    def local_sum(zz):
        slot = zz * 2 + x
        core_copy(slot).wait_recv()
        x_copy(zz).wait_recv()
        main = (
            own_part(rep(zz, x, c))
            + core_in[slot, body_rows].astype(F32)
            + x_in[zz, body_rows].astype(F32)
        )
        flag = (
            flags + core_in[slot, flag_rows].astype(F32) + x_in[zz, flag_rows].astype(F32)
        )
        return main, flag

    def put(dst, zz, main, flag):
        dst[zz, body_rows] = main.astype(BF16)
        dst[zz, flag_rows] = flag.astype(BF16)

    def plus(pair, src, zz):
        return (
            pair[0] + src[zz, body_rows].astype(F32),
            pair[1] + src[zz, flag_rows].astype(F32),
        )

    def sum_z(i):
        zz = jnp.where(z < depth // 2, depth - 1 - order(i), order(i))

        @pl.when(zz > z)
        def _():
            pair = local_sum(zz)

            @pl.when(z == 0)
            def _():
                put(z_out, zz, *pair)

            @pl.when(z > 0)
            def _():
                up_copy(zz).wait_recv()
                put(z_out, zz, *plus(pair, up_in, zz))

            up_copy(zz).start()

        @pl.when(zz < z)
        def _():
            pair = local_sum(zz)

            @pl.when(z == depth - 1)
            def _():
                put(z_out, zz, *pair)

            @pl.when(z < depth - 1)
            def _():
                down_copy(zz).wait_recv()
                put(z_out, zz, *plus(pair, down_in, zz))

            down_copy(zz).start()

    def sum_end():
        main, flag = local_sum(z)
        part[pl.ds(0, rows)] = main
        part[pl.ds(rows, FLAG_ROWS)] = flag

        def add(src, copy):
            copy(z).wait_recv()
            part[pl.ds(0, rows)] += src[z, body_rows].astype(F32)
            part[pl.ds(rows, FLAG_ROWS)] += src[z, flag_rows].astype(F32)

        pl.when(z > 0)(lambda: add(up_in, up_copy))
        pl.when(z < depth - 1)(lambda: add(down_in, down_copy))
        weight_grad_ref[...] = part[pl.ds(0, rows)] / part[pl.ds(rows, 1)]

    def columns(zz):
        return pl.ds(pl.multiple_of(zz * group, group), group)

    def grad_group(d):
        def body(zz, _):
            core_wait(head, zz)
            mixed_grad[...] += dot(cot[:, columns(zz)], w_all[head, columns(zz)], (1, 0))

        around(d, body)

    def layer_copy(zz):
        return pltpu.make_async_copy(
            layer.at[:, columns(zz)], layer_hbm.at[0, :, columns(zz)], layer_sem.at[zz]
        )

    def term(hh, zz):
        return dot(mixed_all[hh], w_all[hh, columns(zz)], (1, 1)).astype(BF16).astype(F32)

    def layer_group(d):
        def body(zz, _):
            each(heads - 1, lambda j: core_wait(peer(j), zz))
            total = term(0, zz)
            if heads <= 4:
                for i in range(1, heads):
                    total = total + term(i, zz)
            else:
                total = lax.fori_loop(1, heads, lambda i, t: t + term(i, zz), total)
            layer[:, columns(zz)] = total.astype(BF16)
            layer_copy(zz).start()

        around(d, body)

    each(depth, sum_start)
    gather_z(1)
    gather_x(0)
    for i in range(depth):
        sum_x(i)
        if i + 2 < depth:
            gather_z(i + 2)
        if i + 1 < depth:
            gather_x(i + 1)
    mixed_grad[...] = jnp.zeros_like(mixed_grad)
    loads[4].wait()
    for i in range(depth):
        gather_heads(i)
        sum_z(i)
        grad_group(i)
        if i == 0:
            each(heads - 1, mixed_wait)
        if i > 0:
            layer_group(i - 1)
    value_grad_ref[0] = dot(
        weights_ref[...], mixed_grad[...].astype(BF16), (0, 0)
    ).astype(BF16)
    layer_group(depth - 1)
    sum_end()

    each(depth, lambda i: layer_copy(i).wait())
    each(heads - 1, lambda j: mixed_copy(j).wait_send())

    def drain(zz):
        for xx in (0, 1):
            rr = rep(zz, xx, c)
            each(heads - 1, lambda j: to_peer(j, rr).wait_send())
            each(heads, lambda hh: to_core(hh, rr).wait_send())
            core_copy(zz * 2 + xx).wait_send()
        rr = rep(zz, x, c)
        to_across(rr).wait_send()
        x_copy(zz).wait_send()
        pl.when((zz <= z) & (z < depth - 1))(lambda: to_above(rr).wait_send())
        pl.when((zz >= z) & (z > 0))(lambda: to_below(rr).wait_send())
        pl.when(zz > z)(lambda: up_copy(zz).wait_send())
        pl.when(zz < z)(lambda: down_copy(zz).wait_send())

    each(depth, drain)


def local(heads, replicas, queries, keys, values, out_weight, cotangent, on_time):
    _, tokens, features = queries.shape
    value_features = values.shape[2]
    rows = out_weight.shape[0]
    model = cotangent.shape[2]
    depth = replicas // 4
    summed = (rows + FLAG_ROWS, value_features)
    any_spec = pl.BlockSpec(memory_space=pl.ANY)
    vmem = pl.BlockSpec(memory_space=pltpu.VMEM)
    dma = pltpu.SemaphoreType.DMA
    return pl.pallas_call(
        functools.partial(kernel, heads, replicas),
        out_shape=(
            jax.ShapeDtypeStruct(cotangent.shape, BF16),
            jax.ShapeDtypeStruct(values.shape, BF16),
            jax.ShapeDtypeStruct(out_weight.shape, F32),
        ),
        in_specs=[any_spec] * 5 + [pl.BlockSpec(memory_space=pltpu.SMEM)],
        out_specs=(any_spec, vmem, vmem),
        scratch_shapes=[
            pltpu.VMEM((tokens, features), BF16),
            pltpu.VMEM((tokens, features), BF16),
            pltpu.VMEM((tokens, value_features), BF16),
            pltpu.VMEM((tokens, model), BF16),
            pltpu.VMEM((tokens, model), BF16),
            pltpu.VMEM((heads, model, value_features), BF16),
            pltpu.VMEM((heads, tokens, value_features), BF16),
            pltpu.VMEM((tokens, value_features), F32),
            pltpu.VMEM((model, value_features), F32),
            pltpu.VMEM((tokens, tokens), BF16),
            pltpu.VMEM((depth * 2,) + summed, BF16),
            pltpu.VMEM((depth * 2,) + summed, BF16),
            pltpu.VMEM((depth,) + summed, BF16),
            pltpu.VMEM((depth,) + summed, BF16),
            pltpu.VMEM((depth,) + summed, BF16),
            pltpu.VMEM((depth,) + summed, BF16),
            pltpu.VMEM((depth,) + summed, BF16),
            dma((5,)),
            dma((depth,)),
            dma((heads, replicas)),
            dma((replicas,)),
            dma((replicas,)),
            dma((replicas,)),
            dma((heads, replicas)),
            dma((heads, replicas)),
            dma((heads,)),
            dma((heads,)),
            dma((depth * 2,)),
            dma((depth * 2,)),
            dma((depth,)),
            dma((depth,)),
            dma((depth,)),
            dma((depth,)),
            dma((depth,)),
        ],
        compiler_params=pltpu.CompilerParams(
            collective_id=0, has_side_effects=True, vmem_limit_bytes=48 * 1024 * 1024
        ),
    )(queries, keys, values, out_weight, cotangent, on_time)


def solution(mesh):
    return jax.shard_map(
        functools.partial(local, mesh.shape["head"], mesh.shape["replica"]),
        mesh=mesh,
        in_specs=(
            P("replica", None, "head"),
            P("replica", None, "head"),
            P("replica", None, "head"),
            P("replica", "head"),
            P("replica", None, None),
            P("replica"),
        ),
        out_specs=(P("replica", None, None), P("replica", None, "head"), P("replica", "head")),
        check_vma=False,
    )
```

time: 204 us -> 50.3 us (0.25)
  waiting for transfers between devices: 161 us -> 0 us
  Pallas kernels: 0 us -> 40.9 us
  between operations: 15.2 us -> 1.3 us
  matrix products: 12 us -> 0 us
  blocking collectives: 10.8 us -> 0 us
  local copies, waits for them, and re-layouts: 3.97 us -> 7.88 us
    psum x1 -> x0, waiting for transfers between devices: 63.2 us -> none  [local(): layer_out = lax.psum(term.astype(jnp.bfloat16), 'head')]
    reduce_scatter x1 -> x0, waiting for transfers between devices: 56.7 us -> none  [local(): lax.psum_scatter(lax.dot_general(cot_rows, masked, (((0,), (0,)), ((), ()...]
    pallas_call x0 -> x1, Pallas kernels: none -> 40.9 us  [local(): pl.pallas_call(functools.partial(kernel, heads, replicas), out_shape=(jax...]
    all_gather x1 -> x0, waiting for transfers between devices: 40.5 us -> none  [local(): full_weight = lax.all_gather(out_weight, 'replica', axis=0, tiled=True)]
    dot_general x5 -> x0, matrix products: 12 us -> none  [the longest x1 3.65 us: local(): lax.dot_general(mixed, full_weight, (((1,), (1,)), ((), ())), preferred_e...]
    psum x1 -> x0, blocking collectives: 10.8 us -> none  [local(): accepted = lax.psum(on_time, 'replica').astype(jnp.float32)]
    unnamed x4 -> x13, local copies, waits for them, and re-layouts: 3.97 us -> 7.88 us
  transfers between devices with their start and end apart: 3 -> 0, of which waited for: 3 -> 0; matrix products, arithmetic and copies ran while one was open for 7% -> 0% of each run, Pallas kernels for 0% -> 0%
where the time goes in v1:
time: 50.3 us; the launch traced here: 50.1 us
  Pallas kernels  40.9 us (81%)
  local copies, waits for them, and re-layouts  7.88 us (16%)
  between operations  1.3 us (3%)
    pallas_call x1, Pallas kernels, local(): pl.pallas_call(functools.partial(kernel, heads, replicas), out_shape=(jax...  40.9 us
    unnamed x13, local copies, waits for them, and re-layouts  7.88 us

profile of v1, /device:TPU:0, one launch (start us, length us, event | category | flops | bytes accessed | tf_op | source)
XLA Modules:
  0.0 50.1 jit_solution(6185028984806708918)
XLA Ops:
  1.3 0.0 copy-start
  1.3 1.6 %copy-done = bf16[1,256,4096]{2,1,0:T(8,128)(2,1)S(1)} copy-done((bf16[1,256,4096]{2,1,0:T(8,128)(2,1)S(1)}, bf16[1,256,4096]{2,1,0:T(8,128)(2,1)}, u32[]{:S(2)}) %copy-start) | copy-done | bytes 2097176
  2.9 0.0 copy-start.1
  2.9 0.9 %copy-done.1 = bf16[1,256,256]{2,1,0:T(8,128)(2,1)S(1)} copy-done((bf16[1,256,256]{2,1,0:T(8,128)(2,1)S(1)}, bf16[1,256,256]{2,1,0:T(8,128)(2,1)}, u32[]{:S(2)}) %copy-start.1) | copy-done | bytes 131096
  3.8 0.0 copy-start.2
  3.8 0.9 %copy-done.2 = bf16[1,256,256]{2,1,0:T(8,128)(2,1)S(1)} copy-done((bf16[1,256,256]{2,1,0:T(8,128)(2,1)S(1)}, bf16[1,256,256]{2,1,0:T(8,128)(2,1)}, u32[]{:S(2)}) %copy-start.2) | copy-done | bytes 131096
  4.7 0.0 copy-start.3
  4.7 0.9 %copy-done.3 = bf16[1,256,256]{2,1,0:T(8,128)(2,1)S(1)} copy-done((bf16[1,256,256]{2,1,0:T(8,128)(2,1)S(1)}, bf16[1,256,256]{2,1,0:T(8,128)(2,1)}, u32[]{:S(2)}) %copy-start.3) | copy-done | bytes 131096
  5.6 0.0 copy-start.4
  5.6 0.9 %copy-done.4 = bf16[256,256]{1,0:T(8,128)(2,1)S(1)} copy-done((bf16[256,256]{1,0:T(8,128)(2,1)S(1)}, bf16[256,256]{1,0:T(8,128)(2,1)}, u32[]{:S(2)}) %copy-start.4) | copy-done | bytes 131096
  6.5 40.9 %shard_map.85 = (bf16[1,256,4096]{2,1,0:T(8,128)(2,1)S(1)}, bf16[1,256,256]{2,1,0:T(8,128)(2,1)S(1)}, f32[256,256]{1,0:T(8,128)S(1)}) custom-call(bf16[1,256,256]{2,1,0:T(8,128)(2,1)S(1)} %copy-done.1, bf16[1,256,256]{2,1,0:T(8,128)(2,1)S(1)} %copy-done.2, bf16[1,256,256]{2,1,0:T(8,128)(2,1)S(1)} %copy-done.3, bf16[256,256]{1,0:T(8,128)(2,1)S(1)} %copy-done.4, ...), custom_call_target="tpu_custom_call" | custom-call | tf_op jit(solution)/shard_map/pallas_call | solution.py:429
  47.4 1.3 %copy.13 = bf16[1,256,4096]{2,1,0:T(8,128)(2,1)} copy(bf16[1,256,4096]{2,1,0:T(8,128)(2,1)S(1)} %get-tuple-element.6) | data formatting | bytes 4194304
  48.7 0.7 %copy.14 = bf16[1,256,256]{2,1,0:T(8,128)(2,1)} copy(bf16[1,256,256]{2,1,0:T(8,128)(2,1)S(1)} %get-tuple-element.7) | data formatting | bytes 262144
  49.4 0.7 %copy.15 = f32[256,256]{1,0:T(8,128)} copy(f32[256,256]{1,0:T(8,128)S(1)} %get-tuple-element.8) | data formatting | bytes 524288
Async XLA Ops:
  1.3 1.6 %copy-start = (bf16[1,256,4096]{2,1,0:T(8,128)(2,1)S(1)}, bf16[1,256,4096]{2,1,0:T(8,128)(2,1)}, u32[]{:S(2)}) copy-start(bf16[1,256,4096]{2,1,0:T(8,128)(2,1)} %cot_hbm.1) | copy-start | bytes 6291460
  2.9 0.9 %copy-start.1 = (bf16[1,256,256]{2,1,0:T(8,128)(2,1)S(1)}, bf16[1,256,256]{2,1,0:T(8,128)(2,1)}, u32[]{:S(2)}) copy-start(bf16[1,256,256]{2,1,0:T(8,128)(2,1)} %q_hbm.1) | copy-start | bytes 393220
  3.8 0.9 %copy-start.2 = (bf16[1,256,256]{2,1,0:T(8,128)(2,1)S(1)}, bf16[1,256,256]{2,1,0:T(8,128)(2,1)}, u32[]{:S(2)}) copy-start(bf16[1,256,256]{2,1,0:T(8,128)(2,1)} %k_hbm.1) | copy-start | bytes 393220
  4.7 0.9 %copy-start.3 = (bf16[1,256,256]{2,1,0:T(8,128)(2,1)S(1)}, bf16[1,256,256]{2,1,0:T(8,128)(2,1)}, u32[]{:S(2)}) copy-start(bf16[1,256,256]{2,1,0:T(8,128)(2,1)} %v_hbm.1) | copy-start | bytes 393220
  5.6 0.9 %copy-start.4 = (bf16[256,256]{1,0:T(8,128)(2,1)S(1)}, bf16[256,256]{1,0:T(8,128)(2,1)}, u32[]{:S(2)}) copy-start(bf16[256,256]{1,0:T(8,128)(2,1)} %w_hbm.1) | copy-start | bytes 393220

commit v2 on v1

--- a/solution.py
+++ b/solution.py
@@ -143,10 +143,12 @@
                 pl.when(z < depth - 1)(lambda: to_above(rr).start())
             else:
                 pl.when(z > 0)(lambda: to_below(rr).start())
-            to_across(rr).start()
             spread(rr)
 
         around(d, body)
+
+    def send_x(d):
+        around(d, lambda zz, _: to_across(rep(zz, x, c)).start())
 
     def gather_x(d):
         def body(zz, _):
@@ -371,20 +373,28 @@
 
         around(d, body)
 
-    each(depth, sum_start)
-    gather_z(1)
+    for i in range(depth):
+        sum_start(i)
+        if i == 0:
+            gather_z(1)
+        else:
+            sum_x(i - 1)
+        if i == 2:
+            send_x(1)
     gather_x(0)
-    for i in range(depth):
-        sum_x(i)
-        if i + 2 < depth:
-            gather_z(i + 2)
-        if i + 1 < depth:
-            gather_x(i + 1)
+    sum_x(depth - 1)
+    for d in range(2, depth):
+        gather_z(d)
+        send_x(d)
+        gather_x(d - 1)
+        sum_z(d - 2)
     mixed_grad[...] = jnp.zeros_like(mixed_grad)
     loads[4].wait()
+    gather_x(depth - 1)
     for i in range(depth):
         gather_heads(i)
-        sum_z(i)
+        if i < 2:
+            sum_z(depth - 2 + i)
         grad_group(i)
         if i == 0:
             each(heads - 1, mixed_wait)
@@ -416,6 +426,21 @@
     each(depth, drain)
 
 
+def hand_over(pieces, *refs):
+    sems = refs[-1]
+    copies = []
+    for src, dst in zip(refs[:3], refs[3:6]):
+        count = pieces if src.shape[-2] * src.shape[-1] > 65536 * pieces else 1
+        step = src.shape[-2] // count
+        for i in range(count):
+            cut = (0,) * (len(src.shape) - 2) + (pl.ds(i * step, step),)
+            copies.append(pltpu.make_async_copy(src.at[cut], dst.at[cut], sems.at[len(copies)]))
+    for copy in copies:
+        copy.start()
+    for copy in copies:
+        copy.wait()
+
+
 def local(heads, replicas, queries, keys, values, out_weight, cotangent, on_time):
     _, tokens, features = queries.shape
     value_features = values.shape[2]
@@ -423,18 +448,18 @@
     model = cotangent.shape[2]
     depth = replicas // 4
     summed = (rows + FLAG_ROWS, value_features)
-    any_spec = pl.BlockSpec(memory_space=pl.ANY)
+    hbm = pl.BlockSpec(memory_space=pltpu.HBM)
     vmem = pl.BlockSpec(memory_space=pltpu.VMEM)
     dma = pltpu.SemaphoreType.DMA
-    return pl.pallas_call(
+    outputs = pl.pallas_call(
         functools.partial(kernel, heads, replicas),
         out_shape=(
             jax.ShapeDtypeStruct(cotangent.shape, BF16),
             jax.ShapeDtypeStruct(values.shape, BF16),
             jax.ShapeDtypeStruct(out_weight.shape, F32),
         ),
-        in_specs=[any_spec] * 5 + [pl.BlockSpec(memory_space=pltpu.SMEM)],
-        out_specs=(any_spec, vmem, vmem),
+        in_specs=[hbm] * 5 + [pl.BlockSpec(memory_space=pltpu.SMEM)],
+        out_specs=(hbm, vmem, vmem),
         scratch_shapes=[
             pltpu.VMEM((tokens, features), BF16),
             pltpu.VMEM((tokens, features), BF16),
@@ -472,9 +497,17 @@
             dma((depth,)),
         ],
         compiler_params=pltpu.CompilerParams(
-            collective_id=0, has_side_effects=True, vmem_limit_bytes=48 * 1024 * 1024
+            collective_id=0, has_side_effects=True, vmem_limit_bytes=56 * 1024 * 1024
         ),
     )(queries, keys, values, out_weight, cotangent, on_time)
+    return pl.pallas_call(
+        functools.partial(hand_over, 4),
+        out_shape=tuple(jax.ShapeDtypeStruct(o.shape, o.dtype) for o in outputs),
+        in_specs=[hbm] * 3,
+        out_specs=(hbm,) * 3,
+        scratch_shapes=[dma((12,))],
+        compiler_params=pltpu.CompilerParams(vmem_limit_bytes=56 * 1024 * 1024),
+    )(*outputs)
 
 
 def solution(mesh):

time: 50.3 us -> 120 us (2.39)
  Pallas kernels: 40.9 us -> 117 us
  local copies, waits for them, and re-layouts: 7.88 us -> 0 us
    pallas_call x0 -> x1, Pallas kernels: none -> 76.7 us  [local(): pl.pallas_call(functools.partial(hand_over, 4), out_shape=tuple((jax.Shap...]
    unnamed x13 -> x0, local copies, waits for them, and re-layouts: 7.88 us -> none
where the time goes in v2:
time: 120 us; the launch traced here: 119 us
  Pallas kernels  117 us (98%)
  between operations  1.29 us (1%)
    pallas_call x1, Pallas kernels, local(): pl.pallas_call(functools.partial(hand_over, 4), out_shape=tuple((jax.Shap...  76.7 us
    pallas_call x1, Pallas kernels, local(): pl.pallas_call(functools.partial(kernel, heads, replicas), out_shape=(jax...  40.8 us

profile of v2, /device:TPU:0, one launch (start us, length us, event | category | flops | bytes accessed | tf_op | source)
XLA Modules:
  0.0 118.8 jit_solution(12318459374337865726)
XLA Ops:
  1.3 40.8 %shard_map.85 = (bf16[1,256,4096]{2,1,0:T(8,128)(2,1)}, bf16[1,256,256]{2,1,0:T(8,128)(2,1)}, f32[256,256]{1,0:T(8,128)}) custom-call(bf16[1,256,256]{2,1,0:T(8,128)(2,1)} %q_hbm.1, bf16[1,256,256]{2,1,0:T(8,128)(2,1)} %k_hbm.1, bf16[1,256,256]{2,1,0:T(8,128)(2,1)} %v_hbm.1, bf16[256,256]{1,0:T(8,128)(2,1)} %w_hbm.1, bf16[1,256,4096]{2,1,0:T(8,128)(2,1)} %cot_hbm.1, ...), custom_call_target="tpu_custom_call" | custom-call | tf_op jit(solution)/shard_map/pallas_call | solution.py:454
  42.1 76.7 %shard_map.86 = (bf16[1,256,4096]{2,1,0:T(8,128)(2,1)}, bf16[1,256,256]{2,1,0:T(8,128)(2,1)}, f32[256,256]{1,0:T(8,128)}) custom-call(bf16[1,256,4096]{2,1,0:T(8,128)(2,1)} %get-tuple-element.6.refs_0_, bf16[1,256,256]{2,1,0:T(8,128)(2,1)} %get-tuple-element.7.refs_1_, f32[256,256]{1,0:T(8,128)} %get-tuple-element.8.refs_2_), custom_call_target="tpu_custom_call" | custom-call | tf_op jit(solution)/shard_map/pallas_call | solution.py:503

commit v3 on v2

--- a/solution.py
+++ b/solution.py
@@ -91,9 +91,9 @@
     def block(hh, rr):
         return w_all.at[hh, pl.ds(pl.multiple_of(rr * rows, rows), rows)]
 
-    def w_copy(hh, rr, sem, device, src=None):
+    def w_copy(hh, rr, sem, device):
         return pltpu.make_async_remote_copy(
-            src_ref=block(hh, rr) if src is None else src,
+            src_ref=block(hh, rr),
             dst_ref=block(hh, rr),
             send_sem=sem,
             recv_sem=w_recv.at[hh, rr],
@@ -104,29 +104,36 @@
     def w_wait(hh, rr):
         w_copy(hh, rr, core_send.at[hh, rr], sibling).wait_recv()
 
-    def to_above(rr, src=None):
-        return w_copy(head, rr, up_send.at[rr], above, src)
-
-    def to_below(rr, src=None):
-        return w_copy(head, rr, down_send.at[rr], below, src)
-
-    def to_across(rr, src=None):
-        return w_copy(head, rr, x_send.at[rr], across, src)
-
-    def to_peer(j, rr, src=None):
-        return w_copy(head, rr, head_send.at[j, rr], (peer(j), me), src)
-
-    def to_core(hh, rr, src=None):
-        return w_copy(hh, rr, core_send.at[hh, rr], sibling, src)
-
-    def spread(rr, src=None):
-        each(heads - 1, lambda j: to_peer(j, rr, src).start())
-        to_core(head, rr, src).start()
-
-    pl.when(z < depth - 1)(lambda: to_above(me, w_hbm).start())
-    pl.when(z > 0)(lambda: to_below(me, w_hbm).start())
-    to_across(me, w_hbm).start()
-    spread(me, w_hbm)
+    def to_above(hh, rr):
+        return w_copy(hh, rr, up_send.at[hh, rr], above)
+
+    def to_below(hh, rr):
+        return w_copy(hh, rr, down_send.at[hh, rr], below)
+
+    def to_across(rr):
+        return w_copy(head, rr, x_send.at[rr], across)
+
+    def to_peer(j, rr):
+        return w_copy(head, rr, head_send.at[j, rr], (peer(j), me))
+
+    def to_core(hh, rr):
+        return w_copy(hh, rr, core_send.at[hh, rr], sibling)
+
+    def to_peers(rr):
+        each(heads - 1, lambda j: to_peer(j, rr).start())
+
+    def send_up(hh, rr):
+        pl.when(z < depth - 1)(lambda: to_above(hh, rr).start())
+
+    def send_down(hh, rr):
+        pl.when(z > 0)(lambda: to_below(hh, rr).start())
+
+    loads[4].wait()
+    send_up(head, me)
+    send_down(head, me)
+    to_peers(me)
+    to_across(me).start()
+    to_core(head, me).start()
 
     def around(d, body):
         if isinstance(d, int) and d == 0:
@@ -135,15 +142,30 @@
             pl.when(z - d >= 0)(lambda: body(z - d, True))
             pl.when(z + d < depth)(lambda: body(z + d, False))
 
+    def gather_y():
+        def body(j):
+            hh = peer(j)
+            w_wait(hh, me)
+            send_up(hh, me)
+            send_down(hh, me)
+            to_core(hh, me).start()
+
+        each(heads - 1, body)
+
     def gather_z(d):
         def body(zz, went_up):
             rr = rep(zz, x, c)
-            w_wait(head, rr)
-            if went_up:
-                pl.when(z < depth - 1)(lambda: to_above(rr).start())
-            else:
-                pl.when(z > 0)(lambda: to_below(rr).start())
-            spread(rr)
+
+            def one(j):
+                hh = lax.rem(head + j, heads)
+                w_wait(hh, rr)
+                if went_up:
+                    send_up(hh, rr)
+                else:
+                    send_down(hh, rr)
+                to_core(hh, rr).start()
+
+            each(heads, one)
 
         around(d, body)
 
@@ -154,17 +176,18 @@
         def body(zz, _):
             rr = rep(zz, 1 - x, c)
             w_wait(head, rr)
-            spread(rr)
+            to_peers(rr)
+            to_core(head, rr).start()
 
         around(d, body)
 
     def gather_heads(d):
         def body(zz, _):
+            rr = rep(zz, 1 - x, c)
+
             def from_peer(j):
-                for xx in (x, 1 - x):
-                    rr = rep(zz, xx, c)
-                    w_wait(peer(j), rr)
-                    to_core(peer(j), rr).start()
+                w_wait(peer(j), rr)
+                to_core(peer(j), rr).start()
 
             each(heads - 1, from_peer)
 
@@ -373,30 +396,30 @@
 
         around(d, body)
 
+    gather_y()
+    gather_z(1)
     for i in range(depth):
         sum_start(i)
-        if i == 0:
-            gather_z(1)
-        else:
+        if i == 1:
+            gather_x(0)
+        if i > 0:
             sum_x(i - 1)
         if i == 2:
             send_x(1)
-    gather_x(0)
     sum_x(depth - 1)
+    mixed_grad[...] = jnp.zeros_like(mixed_grad)
     for d in range(2, depth):
         gather_z(d)
+        sum_z(d - 2)
+        gather_x(d - 1)
         send_x(d)
-        gather_x(d - 1)
-        sum_z(d - 2)
-    mixed_grad[...] = jnp.zeros_like(mixed_grad)
-    loads[4].wait()
-    gather_x(depth - 1)
     for i in range(depth):
         gather_heads(i)
+        grad_group(i)
         if i < 2:
             sum_z(depth - 2 + i)
-        grad_group(i)
         if i == 0:
+            gather_x(depth - 1)
             each(heads - 1, mixed_wait)
         if i > 0:
             layer_group(i - 1)
@@ -410,35 +433,48 @@
     each(heads - 1, lambda j: mixed_copy(j).wait_send())
 
     def drain(zz):
-        for xx in (0, 1):
-            rr = rep(zz, xx, c)
-            each(heads - 1, lambda j: to_peer(j, rr).wait_send())
-            each(heads, lambda hh: to_core(hh, rr).wait_send())
-            core_copy(zz * 2 + xx).wait_send()
         rr = rep(zz, x, c)
+        far = rep(zz, 1 - x, c)
+
+        def one(hh):
+            to_core(hh, rr).wait_send()
+            to_core(hh, far).wait_send()
+            pl.when((zz <= z) & (z < depth - 1))(lambda: to_above(hh, rr).wait_send())
+            pl.when((zz >= z) & (z > 0))(lambda: to_below(hh, rr).wait_send())
+
+        each(heads, one)
+        each(heads - 1, lambda j: to_peer(j, far).wait_send())
         to_across(rr).wait_send()
+        core_copy(zz * 2).wait_send()
+        core_copy(zz * 2 + 1).wait_send()
         x_copy(zz).wait_send()
-        pl.when((zz <= z) & (z < depth - 1))(lambda: to_above(rr).wait_send())
-        pl.when((zz >= z) & (z > 0))(lambda: to_below(rr).wait_send())
         pl.when(zz > z)(lambda: up_copy(zz).wait_send())
         pl.when(zz < z)(lambda: down_copy(zz).wait_send())
 
+    each(heads - 1, lambda j: to_peer(j, me).wait_send())
     each(depth, drain)
 
 
 def hand_over(pieces, *refs):
-    sems = refs[-1]
-    copies = []
-    for src, dst in zip(refs[:3], refs[3:6]):
+    load_sem, store_sem = refs[-2:]
+    moves = []
+    for src, dst, held in zip(refs[:3], refs[3:6], refs[6:9]):
         count = pieces if src.shape[-2] * src.shape[-1] > 65536 * pieces else 1
         step = src.shape[-2] // count
         for i in range(count):
             cut = (0,) * (len(src.shape) - 2) + (pl.ds(i * step, step),)
-            copies.append(pltpu.make_async_copy(src.at[cut], dst.at[cut], sems.at[len(copies)]))
-    for copy in copies:
-        copy.start()
-    for copy in copies:
-        copy.wait()
+            n = len(moves)
+            moves.append((
+                pltpu.make_async_copy(src.at[cut], held.at[cut], load_sem.at[n]),
+                pltpu.make_async_copy(held.at[cut], dst.at[cut], store_sem.at[n]),
+            ))
+    for load, _ in moves:
+        load.start()
+    for load, store in moves:
+        load.wait()
+        store.start()
+    for _, store in moves:
+        store.wait()
 
 
 def local(heads, replicas, queries, keys, values, out_weight, cotangent, on_time):
@@ -481,8 +517,8 @@
             dma((5,)),
             dma((depth,)),
             dma((heads, replicas)),
-            dma((replicas,)),
-            dma((replicas,)),
+            dma((heads, replicas)),
+            dma((heads, replicas)),
             dma((replicas,)),
             dma((heads, replicas)),
             dma((heads, replicas)),
@@ -501,11 +537,11 @@
         ),
     )(queries, keys, values, out_weight, cotangent, on_time)
     return pl.pallas_call(
-        functools.partial(hand_over, 4),
+        functools.partial(hand_over, 8),
         out_shape=tuple(jax.ShapeDtypeStruct(o.shape, o.dtype) for o in outputs),
         in_specs=[hbm] * 3,
         out_specs=(hbm,) * 3,
-        scratch_shapes=[dma((12,))],
+        scratch_shapes=[pltpu.VMEM(o.shape, o.dtype) for o in outputs] + [dma((10,)), dma((10,))],
         compiler_params=pltpu.CompilerParams(vmem_limit_bytes=56 * 1024 * 1024),
     )(*outputs)
 

time: 120 us -> 54 us (0.45)
  Pallas kernels: 117 us -> 52.5 us
    pallas_call x1, Pallas kernels: 76.7 us -> 2.56 us  [local(): pl.pallas_call(functools.partial(hand_over, 8), out_shape=tuple((jax.Shap...]
    pallas_call x1, Pallas kernels: 40.8 us -> 50 us  [local(): pl.pallas_call(functools.partial(kernel, heads, replicas), out_shape=(jax...]
where the time goes in v3:
time: 54 us; the launch traced here: 53.8 us
  Pallas kernels  52.5 us (97%)
  between operations  1.29 us (2%)
    pallas_call x1, Pallas kernels, local(): pl.pallas_call(functools.partial(kernel, heads, replicas), out_shape=(jax...  50 us
    pallas_call x1, Pallas kernels, local(): pl.pallas_call(functools.partial(hand_over, 8), out_shape=tuple((jax.Shap...  2.56 us

profile of v3, /device:TPU:0, one launch (start us, length us, event | category | flops | bytes accessed | tf_op | source)
XLA Modules:
  0.0 53.8 jit_solution(7722215027102716293)
XLA Ops:
  1.3 50.0 %shard_map.85 = (bf16[1,256,4096]{2,1,0:T(8,128)(2,1)}, bf16[1,256,256]{2,1,0:T(8,128)(2,1)}, f32[256,256]{1,0:T(8,128)}) custom-call(bf16[1,256,256]{2,1,0:T(8,128)(2,1)} %q_hbm.1, bf16[1,256,256]{2,1,0:T(8,128)(2,1)} %k_hbm.1, bf16[1,256,256]{2,1,0:T(8,128)(2,1)} %v_hbm.1, bf16[256,256]{1,0:T(8,128)(2,1)} %w_hbm.1, bf16[1,256,4096]{2,1,0:T(8,128)(2,1)} %cot_hbm.1, ...), custom_call_target="tpu_custom_call" | custom-call | tf_op jit(solution)/shard_map/pallas_call | solution.py:490
  51.2 2.6 %shard_map.86 = (bf16[1,256,4096]{2,1,0:T(8,128)(2,1)}, bf16[1,256,256]{2,1,0:T(8,128)(2,1)}, f32[256,256]{1,0:T(8,128)}) custom-call(bf16[1,256,4096]{2,1,0:T(8,128)(2,1)} %get-tuple-element.6.refs_0_, bf16[1,256,256]{2,1,0:T(8,128)(2,1)} %get-tuple-element.7.refs_1_, f32[256,256]{1,0:T(8,128)} %get-tuple-element.8.refs_2_), custom_call_target="tpu_custom_call" | custom-call | tf_op jit(solution)/shard_map/pallas_call | solution.py:539

commit v4 on v3

--- a/solution.py
+++ b/solution.py
@@ -39,11 +39,11 @@
     q_hbm, k_hbm, v_hbm, w_hbm, cot_hbm, on_ref,
     layer_hbm, value_grad_ref, weight_grad_ref,
     q, k, v, cot, layer, w_all, mixed_all, mixed_grad, part, weights_ref,
-    core_out, core_in, x_out, x_in, z_out, up_in, down_in,
+    core_out, core_in, x_out, x_in, z_out, z_in,
     load_sem, layer_sem,
-    w_recv, up_send, down_send, x_send, head_send, core_send,
+    w_recv, line_send, x_send, head_send, core_send,
     mixed_send, mixed_recv,
-    core_out_sem, core_in_sem, x_out_sem, x_in_sem, z_out_sem, up_sem, down_sem,
+    core_out_sem, core_in_sem, x_out_sem, x_in_sem, z_out_sem, z_in_sem,
 ):
     depth = replicas // 4
     rows = w_hbm.shape[0]
@@ -58,8 +58,9 @@
 
     sibling = (head, rep(z, x, 1 - c))
     across = (head, rep(z, 1 - x, c))
-    above = (head, rep(z + 1, x, c))
-    below = (head, rep(z - 1, x, c))
+
+    def line(zz):
+        return (head, rep(zz, x, c))
 
     def peer(j):
         return lax.rem(head + 1 + j, heads)
@@ -72,8 +73,7 @@
     greet(sibling)
     greet(across)
     each(heads - 1, lambda j: greet((peer(j), me)))
-    pl.when(z > 0)(lambda: greet(below))
-    pl.when(z < depth - 1)(lambda: greet(above))
+    each(depth, lambda zz: pl.when(zz != z)(lambda: greet(line(zz))))
 
     loads = [
         pltpu.make_async_copy(src, dst, load_sem.at[i])
@@ -84,9 +84,7 @@
     ]
     for load in loads:
         load.start()
-    pl.semaphore_wait(
-        barrier, 1 + heads + jnp.where(z > 0, 1, 0) + jnp.where(z < depth - 1, 1, 0)
-    )
+    pl.semaphore_wait(barrier, heads + depth)
 
     def block(hh, rr):
         return w_all.at[hh, pl.ds(pl.multiple_of(rr * rows, rows), rows)]
@@ -104,11 +102,8 @@
     def w_wait(hh, rr):
         w_copy(hh, rr, core_send.at[hh, rr], sibling).wait_recv()
 
-    def to_above(hh, rr):
-        return w_copy(hh, rr, up_send.at[hh, rr], above)
-
-    def to_below(hh, rr):
-        return w_copy(hh, rr, down_send.at[hh, rr], below)
+    def to_line(zz):
+        return w_copy(head, me, line_send.at[zz], line(zz))
 
     def to_across(rr):
         return w_copy(head, rr, x_send.at[rr], across)
@@ -122,58 +117,34 @@
     def to_peers(rr):
         each(heads - 1, lambda j: to_peer(j, rr).start())
 
-    def send_up(hh, rr):
-        pl.when(z < depth - 1)(lambda: to_above(hh, rr).start())
-
-    def send_down(hh, rr):
-        pl.when(z > 0)(lambda: to_below(hh, rr).start())
+    def around(d, body):
+        if isinstance(d, int) and d == 0:
+            body(z)
+        else:
+            pl.when(z - d >= 0)(lambda: body(z - d))
+            pl.when(z + d < depth)(lambda: body(z + d))
+
+    def send_line(d):
+        around(d, lambda zz: to_line(zz).start())
 
     loads[4].wait()
-    send_up(head, me)
-    send_down(head, me)
+    send_line(1)
     to_peers(me)
     to_across(me).start()
     to_core(head, me).start()
 
-    def around(d, body):
-        if isinstance(d, int) and d == 0:
-            body(z, None)
-        else:
-            pl.when(z - d >= 0)(lambda: body(z - d, True))
-            pl.when(z + d < depth)(lambda: body(z + d, False))
-
-    def gather_y():
-        def body(j):
-            hh = peer(j)
-            w_wait(hh, me)
-            send_up(hh, me)
-            send_down(hh, me)
-            to_core(hh, me).start()
-
-        each(heads - 1, body)
-
     def gather_z(d):
-        def body(zz, went_up):
+        def body(zz):
             rr = rep(zz, x, c)
-
-            def one(j):
-                hh = lax.rem(head + j, heads)
-                w_wait(hh, rr)
-                if went_up:
-                    send_up(hh, rr)
-                else:
-                    send_down(hh, rr)
-                to_core(hh, rr).start()
-
-            each(heads, one)
+            w_wait(head, rr)
+            to_peers(rr)
+            to_across(rr).start()
+            to_core(head, rr).start()
 
         around(d, body)
 
-    def send_x(d):
-        around(d, lambda zz, _: to_across(rep(zz, x, c)).start())
-
     def gather_x(d):
-        def body(zz, _):
+        def body(zz):
             rr = rep(zz, 1 - x, c)
             w_wait(head, rr)
             to_peers(rr)
@@ -182,12 +153,11 @@
         around(d, body)
 
     def gather_heads(d):
-        def body(zz, _):
-            rr = rep(zz, 1 - x, c)
-
+        def body(zz):
             def from_peer(j):
-                w_wait(peer(j), rr)
-                to_core(peer(j), rr).start()
+                for xx in (x, 1 - x):
+                    w_wait(peer(j), rep(zz, xx, c))
+                    to_core(peer(j), rep(zz, xx, c)).start()
 
             each(heads - 1, from_peer)
 
@@ -258,16 +228,10 @@
             device_id=across, device_id_type=MESH,
         )
 
-    def up_copy(zz):
+    def z_copy(zz, source, other):
         return pltpu.make_async_remote_copy(
-            z_out.at[zz], up_in.at[zz], z_out_sem.at[zz], up_sem.at[zz],
-            device_id=above, device_id_type=MESH,
-        )
-
-    def down_copy(zz):
-        return pltpu.make_async_remote_copy(
-            z_out.at[zz], down_in.at[zz], z_out_sem.at[zz], down_sem.at[zz],
-            device_id=below, device_id_type=MESH,
+            z_out.at[zz], z_in.at[source], z_out_sem.at[zz], z_in_sem.at[source],
+            device_id=line(other), device_id_type=MESH,
         )
 
     loads[3].wait()
@@ -307,68 +271,36 @@
         )
         return main, flag
 
-    def put(dst, zz, main, flag):
-        dst[zz, body_rows] = main.astype(BF16)
-        dst[zz, flag_rows] = flag.astype(BF16)
-
-    def plus(pair, src, zz):
-        return (
-            pair[0] + src[zz, body_rows].astype(F32),
-            pair[1] + src[zz, flag_rows].astype(F32),
-        )
-
     def sum_z(i):
-        zz = jnp.where(z < depth // 2, depth - 1 - order(i), order(i))
-
-        @pl.when(zz > z)
+        zz = order(i)
+
+        @pl.when(zz != z)
         def _():
-            pair = local_sum(zz)
-
-            @pl.when(z == 0)
-            def _():
-                put(z_out, zz, *pair)
-
-            @pl.when(z > 0)
-            def _():
-                up_copy(zz).wait_recv()
-                put(z_out, zz, *plus(pair, up_in, zz))
-
-            up_copy(zz).start()
-
-        @pl.when(zz < z)
-        def _():
-            pair = local_sum(zz)
-
-            @pl.when(z == depth - 1)
-            def _():
-                put(z_out, zz, *pair)
-
-            @pl.when(z < depth - 1)
-            def _():
-                down_copy(zz).wait_recv()
-                put(z_out, zz, *plus(pair, down_in, zz))
-
-            down_copy(zz).start()
+            main, flag = local_sum(zz)
+            z_out[zz, body_rows] = main.astype(BF16)
+            z_out[zz, flag_rows] = flag.astype(BF16)
+            z_copy(zz, z, zz).start()
 
     def sum_end():
         main, flag = local_sum(z)
         part[pl.ds(0, rows)] = main
         part[pl.ds(rows, FLAG_ROWS)] = flag
 
-        def add(src, copy):
-            copy(z).wait_recv()
-            part[pl.ds(0, rows)] += src[z, body_rows].astype(F32)
-            part[pl.ds(rows, FLAG_ROWS)] += src[z, flag_rows].astype(F32)
-
-        pl.when(z > 0)(lambda: add(up_in, up_copy))
-        pl.when(z < depth - 1)(lambda: add(down_in, down_copy))
+        def add(source):
+            @pl.when(source != z)
+            def _():
+                z_copy(z, source, source).wait_recv()
+                part[pl.ds(0, rows)] += z_in[source, body_rows].astype(F32)
+                part[pl.ds(rows, FLAG_ROWS)] += z_in[source, flag_rows].astype(F32)
+
+        each(depth, add)
         weight_grad_ref[...] = part[pl.ds(0, rows)] / part[pl.ds(rows, 1)]
 
     def columns(zz):
         return pl.ds(pl.multiple_of(zz * group, group), group)
 
     def grad_group(d):
-        def body(zz, _):
+        def body(zz):
             core_wait(head, zz)
             mixed_grad[...] += dot(cot[:, columns(zz)], w_all[head, columns(zz)], (1, 0))
 
@@ -383,7 +315,7 @@
         return dot(mixed_all[hh], w_all[hh, columns(zz)], (1, 1)).astype(BF16).astype(F32)
 
     def layer_group(d):
-        def body(zz, _):
+        def body(zz):
             each(heads - 1, lambda j: core_wait(peer(j), zz))
             total = term(0, zz)
             if heads <= 4:
@@ -396,7 +328,8 @@
 
         around(d, body)
 
-    gather_y()
+    for d in range(2, depth):
+        send_line(d)
     gather_z(1)
     for i in range(depth):
         sum_start(i)
@@ -404,30 +337,27 @@
             gather_x(0)
         if i > 0:
             sum_x(i - 1)
-        if i == 2:
-            send_x(1)
     sum_x(depth - 1)
     mixed_grad[...] = jnp.zeros_like(mixed_grad)
     for d in range(2, depth):
         gather_z(d)
         sum_z(d - 2)
         gather_x(d - 1)
-        send_x(d)
+    sum_z(depth - 2)
+    sum_z(depth - 1)
+    each(heads - 1, mixed_wait)
     for i in range(depth):
         gather_heads(i)
         grad_group(i)
-        if i < 2:
-            sum_z(depth - 2 + i)
         if i == 0:
             gather_x(depth - 1)
-            each(heads - 1, mixed_wait)
-        if i > 0:
-            layer_group(i - 1)
+        if i < depth - 1:
+            layer_group(i)
     value_grad_ref[0] = dot(
         weights_ref[...], mixed_grad[...].astype(BF16), (0, 0)
     ).astype(BF16)
+    sum_end()
     layer_group(depth - 1)
-    sum_end()
 
     each(depth, lambda i: layer_copy(i).wait())
     each(heads - 1, lambda j: mixed_copy(j).wait_send())
@@ -439,19 +369,20 @@
         def one(hh):
             to_core(hh, rr).wait_send()
             to_core(hh, far).wait_send()
-            pl.when((zz <= z) & (z < depth - 1))(lambda: to_above(hh, rr).wait_send())
-            pl.when((zz >= z) & (z > 0))(lambda: to_below(hh, rr).wait_send())
 
         each(heads, one)
+        each(heads - 1, lambda j: to_peer(j, rr).wait_send())
         each(heads - 1, lambda j: to_peer(j, far).wait_send())
         to_across(rr).wait_send()
         core_copy(zz * 2).wait_send()
         core_copy(zz * 2 + 1).wait_send()
         x_copy(zz).wait_send()
-        pl.when(zz > z)(lambda: up_copy(zz).wait_send())
-        pl.when(zz < z)(lambda: down_copy(zz).wait_send())
-
-    each(heads - 1, lambda j: to_peer(j, me).wait_send())
+
+        @pl.when(zz != z)
+        def _():
+            to_line(zz).wait_send()
+            z_copy(zz, z, zz).wait_send()
+
     each(depth, drain)
 
 
@@ -513,12 +444,10 @@
             pltpu.VMEM((depth,) + summed, BF16),
             pltpu.VMEM((depth,) + summed, BF16),
             pltpu.VMEM((depth,) + summed, BF16),
-            pltpu.VMEM((depth,) + summed, BF16),
             dma((5,)),
             dma((depth,)),
             dma((heads, replicas)),
-            dma((heads, replicas)),
-            dma((heads, replicas)),
+            dma((depth,)),
             dma((replicas,)),
             dma((heads, replicas)),
             dma((heads, replicas)),
@@ -526,7 +455,6 @@
             dma((heads,)),
             dma((depth * 2,)),
             dma((depth * 2,)),
-            dma((depth,)),
             dma((depth,)),
             dma((depth,)),
             dma((depth,)),

time: 54 us -> 47.3 us (0.88)
  the two profiles are of different devices: /device:TPU:0 before, /device:TPU:21 now
where the time goes in v4:
time: 47.3 us; the launch traced here: 47.1 us
  Pallas kernels  45.8 us (97%)
  between operations  1.29 us (3%)
    pallas_call x1, Pallas kernels, local(): pl.pallas_call(functools.partial(kernel, heads, replicas), out_shape=(jax...  43.3 us
    pallas_call x1, Pallas kernels, local(): pl.pallas_call(functools.partial(hand_over, 8), out_shape=tuple((jax.Shap...  2.56 us

profile of v4, /device:TPU:21, one launch (start us, length us, event | category | flops | bytes accessed | tf_op | source)
XLA Modules:
  0.0 47.1 jit_solution(1036834099431832781)
XLA Ops:
  1.3 43.3 %shard_map.85 = (bf16[1,256,4096]{2,1,0:T(8,128)(2,1)}, bf16[1,256,256]{2,1,0:T(8,128)(2,1)}, f32[256,256]{1,0:T(8,128)}) custom-call(bf16[1,256,256]{2,1,0:T(8,128)(2,1)} %q_hbm.1, bf16[1,256,256]{2,1,0:T(8,128)(2,1)} %k_hbm.1, bf16[1,256,256]{2,1,0:T(8,128)(2,1)} %v_hbm.1, bf16[256,256]{1,0:T(8,128)(2,1)} %w_hbm.1, bf16[1,256,4096]{2,1,0:T(8,128)(2,1)} %cot_hbm.1, ...), custom_call_target="tpu_custom_call" | custom-call | tf_op jit(solution)/shard_map/pallas_call | solution.py:421
  44.6 2.6 %shard_map.86 = (bf16[1,256,4096]{2,1,0:T(8,128)(2,1)}, bf16[1,256,256]{2,1,0:T(8,128)(2,1)}, f32[256,256]{1,0:T(8,128)}) custom-call(bf16[1,256,4096]{2,1,0:T(8,128)(2,1)} %get-tuple-element.6.refs_0_, bf16[1,256,256]{2,1,0:T(8,128)(2,1)} %get-tuple-element.7.refs_1_, f32[256,256]{1,0:T(8,128)} %get-tuple-element.8.refs_2_), custom_call_target="tpu_custom_call" | custom-call | tf_op jit(solution)/shard_map/pallas_call | solution.py:467

commit v5 on v4

--- a/solution.py
+++ b/solution.py
@@ -38,7 +38,7 @@
     heads, replicas,
     q_hbm, k_hbm, v_hbm, w_hbm, cot_hbm, on_ref,
     layer_hbm, value_grad_ref, weight_grad_ref,
-    q, k, v, cot, layer, w_all, mixed_all, mixed_grad, part, weights_ref,
+    q, k, v, cot, layer, w_all, mixed_all, mixed_grad, part, total, weights_ref,
     core_out, core_in, x_out, x_in, z_out, z_in,
     load_sem, layer_sem,
     w_recv, line_send, x_send, head_send, core_send,
@@ -204,18 +204,16 @@
     each(heads - 1, lambda j: mixed_copy(j).start())
 
     on = on_ref[0].astype(F32)
-    flags = jnp.full((FLAG_ROWS, part.shape[1]), 1.0, F32) * on
-    body_rows = pl.ds(0, rows)
-    flag_rows = pl.ds(rows, FLAG_ROWS)
+    features = part.shape[1]
+    flags = jnp.full((FLAG_ROWS, rows), 1.0, F32) * on
+    body_rows = pl.ds(0, features)
+    flag_rows = pl.ds(features, FLAG_ROWS)
 
     def order(i):
         if isinstance(i, int):
             return i // 2 if i % 2 == 0 else depth - 1 - i // 2
         return jnp.where(i % 2 == 0, i // 2, depth - 1 - i // 2)
 
-    def own_part(rr):
-        return part[pl.ds(pl.multiple_of(rr * rows, rows), rows)]
-
     def core_copy(slot):
         return pltpu.make_async_remote_copy(
             core_out.at[slot], core_in.at[slot], core_out_sem.at[slot], core_in_sem.at[slot],
@@ -235,15 +233,18 @@
         )
 
     loads[3].wait()
-    masked = mixed_all[head] * on.astype(BF16)
+    masked_t = dot(v[...], weights_ref[...], (0, 1)).astype(BF16) * on.astype(BF16)
 
     def sum_start(i):
         zz = order(i)
         at = pl.multiple_of(zz * group, group)
-        part[pl.ds(at, group)] = dot(cot[:, pl.ds(at, group)], masked, (0, 0))
-        for xx in (1 - x, x):
+        product = dot(masked_t, cot[:, pl.ds(at, group)], (1, 0))
+        for xx in (0, 1):
             slot = zz * 2 + xx
-            core_out[slot, body_rows] = own_part(rep(zz, xx, 1 - c)).astype(BF16)
+            first = product[:, 2 * xx * rows:(2 * xx + 1) * rows]
+            second = product[:, (2 * xx + 1) * rows:(2 * xx + 2) * rows]
+            part[slot] = jnp.where(c == 0, first, second)
+            core_out[slot, body_rows] = jnp.where(c == 0, second, first).astype(BF16)
             core_out[slot, flag_rows] = flags.astype(BF16)
             core_copy(slot).start()
 
@@ -252,7 +253,7 @@
         slot = zz * 2 + 1 - x
         core_copy(slot).wait_recv()
         x_out[zz, body_rows] = (
-            own_part(rep(zz, 1 - x, c)) + core_in[slot, body_rows].astype(F32)
+            part[slot] + core_in[slot, body_rows].astype(F32)
         ).astype(BF16)
         x_out[zz, flag_rows] = (flags + core_in[slot, flag_rows].astype(F32)).astype(BF16)
         x_copy(zz).start()
@@ -262,7 +263,7 @@
         core_copy(slot).wait_recv()
         x_copy(zz).wait_recv()
         main = (
-            own_part(rep(zz, x, c))
+            part[slot]
             + core_in[slot, body_rows].astype(F32)
             + x_in[zz, body_rows].astype(F32)
         )
@@ -283,18 +284,17 @@
 
     def sum_end():
         main, flag = local_sum(z)
-        part[pl.ds(0, rows)] = main
-        part[pl.ds(rows, FLAG_ROWS)] = flag
+        total[body_rows] = main
+        total[flag_rows] = flag
 
         def add(source):
             @pl.when(source != z)
             def _():
                 z_copy(z, source, source).wait_recv()
-                part[pl.ds(0, rows)] += z_in[source, body_rows].astype(F32)
-                part[pl.ds(rows, FLAG_ROWS)] += z_in[source, flag_rows].astype(F32)
+                total[...] += z_in[source].astype(F32)
 
         each(depth, add)
-        weight_grad_ref[...] = part[pl.ds(0, rows)] / part[pl.ds(rows, 1)]
+        weight_grad_ref[...] = (total[body_rows] / total[pl.ds(features, 1)]).T
 
     def columns(zz):
         return pl.ds(pl.multiple_of(zz * group, group), group)
@@ -333,7 +333,7 @@
     gather_z(1)
     for i in range(depth):
         sum_start(i)
-        if i == 1:
+        if i == 0:
             gather_x(0)
         if i > 0:
             sum_x(i - 1)
@@ -414,7 +414,7 @@
     rows = out_weight.shape[0]
     model = cotangent.shape[2]
     depth = replicas // 4
-    summed = (rows + FLAG_ROWS, value_features)
+    summed = (value_features + FLAG_ROWS, rows)
     hbm = pl.BlockSpec(memory_space=pltpu.HBM)
     vmem = pl.BlockSpec(memory_space=pltpu.VMEM)
     dma = pltpu.SemaphoreType.DMA
@@ -436,7 +436,8 @@
             pltpu.VMEM((heads, model, value_features), BF16),
             pltpu.VMEM((heads, tokens, value_features), BF16),
             pltpu.VMEM((tokens, value_features), F32),
-            pltpu.VMEM((model, value_features), F32),
+            pltpu.VMEM((depth * 2, value_features, rows), F32),
+            pltpu.VMEM(summed, F32),
             pltpu.VMEM((tokens, tokens), BF16),
             pltpu.VMEM((depth * 2,) + summed, BF16),
             pltpu.VMEM((depth * 2,) + summed, BF16),

time: 47.3 us -> 47.3 us (level)
  no operation moved by 1% of the time
where the time goes in v5:
time: 47.3 us; the launch traced here: 47.1 us
  Pallas kernels  45.8 us (97%)
  between operations  1.29 us (3%)
    pallas_call x1, Pallas kernels, local(): pl.pallas_call(functools.partial(kernel, heads, replicas), out_shape=(jax...  43.3 us
    pallas_call x1, Pallas kernels, local(): pl.pallas_call(functools.partial(hand_over, 8), out_shape=tuple((jax.Shap...  2.56 us

profile of v5, /device:TPU:21, one launch (start us, length us, event | category | flops | bytes accessed | tf_op | source)
XLA Modules:
  0.0 47.1 jit_solution(14063657013713467018)
XLA Ops:
  1.3 43.3 %shard_map.85 = (bf16[1,256,4096]{2,1,0:T(8,128)(2,1)}, bf16[1,256,256]{2,1,0:T(8,128)(2,1)}, f32[256,256]{1,0:T(8,128)}) custom-call(bf16[1,256,256]{2,1,0:T(8,128)(2,1)} %q_hbm.1, bf16[1,256,256]{2,1,0:T(8,128)(2,1)} %k_hbm.1, bf16[1,256,256]{2,1,0:T(8,128)(2,1)} %v_hbm.1, bf16[256,256]{1,0:T(8,128)(2,1)} %w_hbm.1, bf16[1,256,4096]{2,1,0:T(8,128)(2,1)} %cot_hbm.1, ...), custom_call_target="tpu_custom_call" | custom-call | tf_op jit(solution)/shard_map/pallas_call | solution.py:421
  44.5 2.6 %shard_map.86 = (bf16[1,256,4096]{2,1,0:T(8,128)(2,1)}, bf16[1,256,256]{2,1,0:T(8,128)(2,1)}, f32[256,256]{1,0:T(8,128)}) custom-call(bf16[1,256,4096]{2,1,0:T(8,128)(2,1)} %get-tuple-element.6.refs_0_, bf16[1,256,256]{2,1,0:T(8,128)(2,1)} %get-tuple-element.7.refs_1_, f32[256,256]{1,0:T(8,128)} %get-tuple-element.8.refs_2_), custom_call_target="tpu_custom_call" | custom-call | tf_op jit(solution)/shard_map/pallas_call | solution.py:468

commit v6 on v5

--- a/solution.py
+++ b/solution.py
@@ -41,7 +41,7 @@
     q, k, v, cot, layer, w_all, mixed_all, mixed_grad, part, total, weights_ref,
     core_out, core_in, x_out, x_in, z_out, z_in,
     load_sem, layer_sem,
-    w_recv, line_send, x_send, head_send, core_send,
+    w_recv, up_send, down_send, partner_send, x_send, head_send, core_send,
     mixed_send, mixed_recv,
     core_out_sem, core_in_sem, x_out_sem, x_in_sem, z_out_sem, z_in_sem,
 ):
@@ -102,8 +102,14 @@
     def w_wait(hh, rr):
         w_copy(hh, rr, core_send.at[hh, rr], sibling).wait_recv()
 
-    def to_line(zz):
-        return w_copy(head, me, line_send.at[zz], line(zz))
+    def to_above(rr):
+        return w_copy(head, rr, up_send.at[rr], line(z + 1))
+
+    def to_below(rr):
+        return w_copy(head, rr, down_send.at[rr], line(z - 1))
+
+    def to_partner(hh, rr):
+        return w_copy(hh, rr, partner_send.at[hh, rr], line(z + 1 - 2 * (z % 2)))
 
     def to_across(rr):
         return w_copy(head, rr, x_send.at[rr], across)
@@ -124,11 +130,9 @@
             pl.when(z - d >= 0)(lambda: body(z - d))
             pl.when(z + d < depth)(lambda: body(z + d))
 
-    def send_line(d):
-        around(d, lambda zz: to_line(zz).start())
-
     loads[4].wait()
-    send_line(1)
+    pl.when(z < depth - 1)(lambda: to_above(me).start())
+    pl.when(z > 0)(lambda: to_below(me).start())
     to_peers(me)
     to_across(me).start()
     to_core(head, me).start()
@@ -137,7 +141,10 @@
         def body(zz):
             rr = rep(zz, x, c)
             w_wait(head, rr)
-            to_peers(rr)
+            pl.when((zz < z) & (z < depth - 1))(lambda: to_above(rr).start())
+            pl.when((zz > z) & (z > 0))(lambda: to_below(rr).start())
+            if d % 2 == 0:
+                to_peers(rr)
             to_across(rr).start()
             to_core(head, rr).start()
 
@@ -152,10 +159,22 @@
 
         around(d, body)
 
+    def gather_y(d):
+        def body(zz):
+            def from_peer(j):
+                rr = rep(zz, x, c)
+                w_wait(peer(j), rr)
+                to_partner(peer(j), rr).start()
+                to_core(peer(j), rr).start()
+
+            each(heads - 1, from_peer)
+
+        around(d, body)
+
     def gather_heads(d):
         def body(zz):
             def from_peer(j):
-                for xx in (x, 1 - x):
+                for xx in (x, 1 - x) if d % 2 else (1 - x,):
                     w_wait(peer(j), rep(zz, xx, c))
                     to_core(peer(j), rep(zz, xx, c)).start()
 
@@ -328,13 +347,12 @@
 
         around(d, body)
 
-    for d in range(2, depth):
-        send_line(d)
     gather_z(1)
     for i in range(depth):
         sum_start(i)
         if i == 0:
             gather_x(0)
+            gather_y(0)
         if i > 0:
             sum_x(i - 1)
     sum_x(depth - 1)
@@ -343,6 +361,8 @@
         gather_z(d)
         sum_z(d - 2)
         gather_x(d - 1)
+        if d % 2:
+            gather_y(d - 1)
     sum_z(depth - 2)
     sum_z(depth - 1)
     each(heads - 1, mixed_wait)
@@ -371,8 +391,18 @@
             to_core(hh, far).wait_send()
 
         each(heads, one)
-        each(heads - 1, lambda j: to_peer(j, rr).wait_send())
         each(heads - 1, lambda j: to_peer(j, far).wait_send())
+
+        @pl.when((zz + z) % 2 == 0)
+        def _():
+            def shared(j):
+                to_peer(j, rr).wait_send()
+                to_partner(peer(j), rr).wait_send()
+
+            each(heads - 1, shared)
+
+        pl.when((zz <= z) & (z < depth - 1))(lambda: to_above(rr).wait_send())
+        pl.when((zz >= z) & (z > 0))(lambda: to_below(rr).wait_send())
         to_across(rr).wait_send()
         core_copy(zz * 2).wait_send()
         core_copy(zz * 2 + 1).wait_send()
@@ -380,7 +410,6 @@
 
         @pl.when(zz != z)
         def _():
-            to_line(zz).wait_send()
             z_copy(zz, z, zz).wait_send()
 
     each(depth, drain)
@@ -448,7 +477,9 @@
             dma((5,)),
             dma((depth,)),
             dma((heads, replicas)),
-            dma((depth,)),
+            dma((replicas,)),
+            dma((replicas,)),
+            dma((heads, replicas)),
             dma((replicas,)),
             dma((heads, replicas)),
             dma((heads, replicas)),

time: 47.3 us -> 44.9 us (0.949)
  the two profiles are of different devices: /device:TPU:21 before, /device:TPU:0 now
where the time goes in v6:
time: 44.9 us; the launch traced here: 44.6 us
  Pallas kernels  43.3 us (96%)
  between operations  1.29 us (3%)
    pallas_call x1, Pallas kernels, local(): pl.pallas_call(functools.partial(kernel, heads, replicas), out_shape=(jax...  40.8 us
    pallas_call x1, Pallas kernels, local(): pl.pallas_call(functools.partial(hand_over, 8), out_shape=tuple((jax.Shap...  2.56 us

profile of v6, /device:TPU:0, one launch (start us, length us, event | category | flops | bytes accessed | tf_op | source)
XLA Modules:
  0.0 44.6 jit_solution(11845351572137165963)
XLA Ops:
  1.3 40.8 %shard_map.85 = (bf16[1,256,4096]{2,1,0:T(8,128)(2,1)}, bf16[1,256,256]{2,1,0:T(8,128)(2,1)}, f32[256,256]{1,0:T(8,128)}) custom-call(bf16[1,256,256]{2,1,0:T(8,128)(2,1)} %q_hbm.1, bf16[1,256,256]{2,1,0:T(8,128)(2,1)} %k_hbm.1, bf16[1,256,256]{2,1,0:T(8,128)(2,1)} %v_hbm.1, bf16[256,256]{1,0:T(8,128)(2,1)} %w_hbm.1, bf16[1,256,4096]{2,1,0:T(8,128)(2,1)} %cot_hbm.1, ...), custom_call_target="tpu_custom_call" | custom-call | tf_op jit(solution)/shard_map/pallas_call | solution.py:450
  42.0 2.6 %shard_map.86 = (bf16[1,256,4096]{2,1,0:T(8,128)(2,1)}, bf16[1,256,256]{2,1,0:T(8,128)(2,1)}, f32[256,256]{1,0:T(8,128)}) custom-call(bf16[1,256,4096]{2,1,0:T(8,128)(2,1)} %get-tuple-element.6.refs_0_, bf16[1,256,256]{2,1,0:T(8,128)(2,1)} %get-tuple-element.7.refs_1_, f32[256,256]{1,0:T(8,128)} %get-tuple-element.8.refs_2_), custom_call_target="tpu_custom_call" | custom-call | tf_op jit(solution)/shard_map/pallas_call | solution.py:499

commit v7 on v6

--- a/solution.py
+++ b/solution.py
@@ -359,23 +359,26 @@
     mixed_grad[...] = jnp.zeros_like(mixed_grad)
     for d in range(2, depth):
         gather_z(d)
+        if d < depth - 1:
+            gather_x(d - 1)
         sum_z(d - 2)
-        gather_x(d - 1)
         if d % 2:
             gather_y(d - 1)
     sum_z(depth - 2)
     sum_z(depth - 1)
+    gather_x(depth - 2)
     each(heads - 1, mixed_wait)
-    for i in range(depth):
+    for i in range(depth - 1):
         gather_heads(i)
         grad_group(i)
         if i == 0:
             gather_x(depth - 1)
-        if i < depth - 1:
-            layer_group(i)
+        layer_group(i)
+    grad_group(depth - 1)
     value_grad_ref[0] = dot(
         weights_ref[...], mixed_grad[...].astype(BF16), (0, 0)
     ).astype(BF16)
+    gather_heads(depth - 1)
     sum_end()
     layer_group(depth - 1)
 

time: 44.9 us -> 44.9 us (level)
  no operation moved by 1% of the time
where the time goes in v7:
time: 44.9 us; the launch traced here: 44.5 us
  Pallas kernels  43.2 us (96%)
  between operations  1.29 us (3%)
    pallas_call x1, Pallas kernels, local(): pl.pallas_call(functools.partial(kernel, heads, replicas), out_shape=(jax...  40.6 us
    pallas_call x1, Pallas kernels, local(): pl.pallas_call(functools.partial(hand_over, 8), out_shape=tuple((jax.Shap...  2.56 us

profile of v7, /device:TPU:0, one launch (start us, length us, event | category | flops | bytes accessed | tf_op | source)
XLA Modules:
  0.0 44.5 jit_solution(2542192399677938436)
XLA Ops:
  1.3 40.6 %shard_map.85 = (bf16[1,256,4096]{2,1,0:T(8,128)(2,1)}, bf16[1,256,256]{2,1,0:T(8,128)(2,1)}, f32[256,256]{1,0:T(8,128)}) custom-call(bf16[1,256,256]{2,1,0:T(8,128)(2,1)} %q_hbm.1, bf16[1,256,256]{2,1,0:T(8,128)(2,1)} %k_hbm.1, bf16[1,256,256]{2,1,0:T(8,128)(2,1)} %v_hbm.1, bf16[256,256]{1,0:T(8,128)(2,1)} %w_hbm.1, bf16[1,256,4096]{2,1,0:T(8,128)(2,1)} %cot_hbm.1, ...), custom_call_target="tpu_custom_call" | custom-call | tf_op jit(solution)/shard_map/pallas_call | solution.py:453
  41.9 2.6 %shard_map.86 = (bf16[1,256,4096]{2,1,0:T(8,128)(2,1)}, bf16[1,256,256]{2,1,0:T(8,128)(2,1)}, f32[256,256]{1,0:T(8,128)}) custom-call(bf16[1,256,4096]{2,1,0:T(8,128)(2,1)} %get-tuple-element.6.refs_0_, bf16[1,256,256]{2,1,0:T(8,128)(2,1)} %get-tuple-element.7.refs_1_, f32[256,256]{1,0:T(8,128)} %get-tuple-element.8.refs_2_), custom_call_target="tpu_custom_call" | custom-call | tf_op jit(solution)/shard_map/pallas_call | solution.py:502

commit v8 on v6

--- a/solution.py
+++ b/solution.py
@@ -82,7 +82,7 @@
              (w_hbm, w_all.at[head, pl.ds(pl.multiple_of(me * rows, rows), rows)]))
         )
     ]
-    for load in loads:
+    for load in [loads[4]] + loads[:4]:
         load.start()
     pl.semaphore_wait(barrier, heads + depth)
 

time: 44.9 us -> 44.9 us (level)
  no operation moved by 1% of the time
where the time goes in v8:
time: 44.9 us; the launch traced here: 44.6 us
  Pallas kernels  43.3 us (96%)
  between operations  1.29 us (3%)
    pallas_call x1, Pallas kernels, local(): pl.pallas_call(functools.partial(kernel, heads, replicas), out_shape=(jax...  40.8 us
    pallas_call x1, Pallas kernels, local(): pl.pallas_call(functools.partial(hand_over, 8), out_shape=tuple((jax.Shap...  2.56 us

profile of v8, /device:TPU:0, one launch (start us, length us, event | category | flops | bytes accessed | tf_op | source)
XLA Modules:
  0.0 44.6 jit_solution(8324641339951178995)
XLA Ops:
  1.3 40.8 %shard_map.85 = (bf16[1,256,4096]{2,1,0:T(8,128)(2,1)}, bf16[1,256,256]{2,1,0:T(8,128)(2,1)}, f32[256,256]{1,0:T(8,128)}) custom-call(bf16[1,256,256]{2,1,0:T(8,128)(2,1)} %q_hbm.1, bf16[1,256,256]{2,1,0:T(8,128)(2,1)} %k_hbm.1, bf16[1,256,256]{2,1,0:T(8,128)(2,1)} %v_hbm.1, bf16[256,256]{1,0:T(8,128)(2,1)} %w_hbm.1, bf16[1,256,4096]{2,1,0:T(8,128)(2,1)} %cot_hbm.1, ...), custom_call_target="tpu_custom_call" | custom-call | tf_op jit(solution)/shard_map/pallas_call | solution.py:450
  42.0 2.6 %shard_map.86 = (bf16[1,256,4096]{2,1,0:T(8,128)(2,1)}, bf16[1,256,256]{2,1,0:T(8,128)(2,1)}, f32[256,256]{1,0:T(8,128)}) custom-call(bf16[1,256,4096]{2,1,0:T(8,128)(2,1)} %get-tuple-element.6.refs_0_, bf16[1,256,256]{2,1,0:T(8,128)(2,1)} %get-tuple-element.7.refs_1_, f32[256,256]{1,0:T(8,128)} %get-tuple-element.8.refs_2_), custom_call_target="tpu_custom_call" | custom-call | tf_op jit(solution)/shard_map/pallas_call | solution.py:499
